TPU v7x, 128 devices: a whole 4x4x4 slice. The times are simulated.
128 devices in a mesh: dp: 2 (over core), context: 16 (over y, x), tensor: 4 (over z).
Axes of the slice: x: 4, y: 4, z: 4, core: 2. Of those that a mesh axis runs over, the one named last changes fastest.
Arguments:
- ids: int32 [16384], P(('dp', 'context', 'tensor')), parts along dimension 0, may hold values from 65 to 84, as said below
- block_order: int32 [64], P('dp'), parts along dimension 0, may hold values from 0 to 31, each once
- embed: bfloat16 [512, 4096], replicated, may hold values from -6 to 6
- mix_gain: float32 [4096], replicated, may hold values from 0.5 to 2
- in_proj: bfloat16 [3, 4096, 2048], P(None, None, 'tensor'), may hold values from -0.09375 to 0.09375
- short_filter: float32 [3, 3, 2048], P(None, None, 'tensor'), may hold values from -1 to 1
- long_filter: float32 [128, 128], P('tensor'), as said below
- conv_skip: float32 [2048], P('tensor'), may hold values from -1 to 1
- hyena_out: bfloat16 [2048, 4096], P('tensor'), may hold values from -0.125 to 0.125
- attn_gain: float32 [4096], replicated, may hold values from 0.5 to 2
- qkv_proj: bfloat16 [3, 4096, 2048], P(None, None, 'tensor'), as said below
- attn_out: bfloat16 [2048, 4096], P('tensor'), may hold values from -0.5 to 0.5
Outputs:
- stream_out: float32 [16384, 4096], P(('dp', 'context', 'tensor')), parts along dimension 0
There are 2 independent parts, one for each index of `dp`. A program takes and returns all parts, laid end to end along the dimension named above; an argument that names none is the same for every part. Nothing has to cross between parts.
Inputs may be any that keep to these rules, and one draw needn't show every extreme that they name: `ids`: every id is the code of a base: 65, 67, 71 or 84. `block_order`: every block lies in exactly one slot. `long_filter`: real-valued filter taps. `qkv_proj`: real-valued projection weights.
All inputs are finite; a program needn't handle non-finite values.
Results may differ from a plain program's by a relative error of at most 0.01.
Values may be sent and summed in bfloat16 or wider, within the bound.
A program may use at most 192 MiB of HBM per device.

v0:
```python
import math
import jax
import jax.numpy as jnp
from jax import lax
from jax.sharding import PartitionSpec as P

HD = 128
GROUP_CH = 16
EPS = 1e-06
THETA = 1000000.0
NEG_FILL = -1e30


def rms_scale(row_data, gain_vec):
    values = row_data.astype(jnp.float32)
    factor = lax.rsqrt(jnp.mean(values * values, axis=-1, keepdims=True) + EPS)
    return (values * factor * gain_vec).astype(jnp.bfloat16)


def toeplitz(long_filter):
    filter_len = long_filter.shape[1]
    tap_lag = (
        jnp.arange(filter_len, dtype=jnp.int32)[:, None]
        - jnp.arange(filter_len, dtype=jnp.int32)[None, :]
    )
    near_taps = jnp.take(long_filter, jnp.clip(tap_lag, 0, filter_len - 1), axis=1)
    far_taps = jnp.take(long_filter, jnp.clip(tap_lag + filter_len, 0, filter_len - 1), axis=1)
    near_taps = jnp.where(tap_lag[None] >= 0, near_taps, jnp.zeros_like(near_taps))
    far_taps = jnp.where(tap_lag[None] < 0, far_taps, jnp.zeros_like(far_taps))
    return (near_taps, far_taps)


def long_conv(padded, long_filter, group_width):
    filter_len = long_filter.shape[1]
    near_taps, far_taps = toeplitz(long_filter)
    row_total = padded.shape[0]
    chan_total = padded.shape[1]
    blocks = padded.reshape(
        row_total // filter_len, filter_len, chan_total // group_width, group_width
    )
    current_part = jnp.einsum(
        "grs,bsgc->brgc", near_taps, blocks[1:], precision=lax.Precision.HIGHEST
    )
    before = jnp.einsum("grs,bsgc->brgc", far_taps, blocks[:-1], precision=lax.Precision.HIGHEST)
    return (current_part + before).reshape(row_total - filter_len, chan_total)


def short_conv(padded_rows, short_filter, out_len):
    taps = short_filter.shape[1]
    result = jnp.zeros((padded_rows.shape[0], out_len, padded_rows.shape[2]), jnp.float32)
    for tap_at in range(taps):
        offset = taps - 1 - tap_at
        result = (
            result + short_filter[:, tap_at][:, None, :] * padded_rows[:, offset : offset + out_len]
        )
    return result


def rotate(values, positions, head_dim):
    half_dim = head_dim // 2
    inverse_freq = THETA ** (-(2.0 * jnp.arange(half_dim, dtype=jnp.float32)) / head_dim)
    angles = positions.astype(jnp.float32)[:, None] * inverse_freq[None, :]
    cosine_part = jnp.cos(angles)[:, None, :]
    sine_part = jnp.sin(angles)[:, None, :]
    lower_half = values[..., :half_dim]
    upper_half = values[..., half_dim:]
    return jnp.concatenate(
        [
            lower_half * cosine_part - upper_half * sine_part,
            upper_half * cosine_part + lower_half * sine_part,
        ],
        axis=-1,
    )


def body(
    ids,
    block_order,
    embed,
    mix_gain,
    in_proj,
    short_filter,
    long_filter,
    conv_skip,
    hyena_out,
    attn_gain,
    qkv_proj,
    attn_out,
):
    tok_rows = ids.shape[0]
    tensor_count = lax.axis_size("tensor")
    context_count = lax.axis_size("context")
    ctx_rows = tok_rows * tensor_count
    block_rows = ctx_rows // 2
    filter_len = long_filter.shape[1]
    short_len = short_filter.shape[1]
    halo_len = filter_len + short_len - 2
    chan_local = in_proj.shape[2]
    context_at = lax.axis_index("context")
    vocab_ids = jnp.arange(embed.shape[0], dtype=jnp.int32)
    chosen = (ids[:, None] == vocab_ids[None, :]).astype(jnp.bfloat16)
    embedded = jnp.dot(chosen, embed, preferred_element_type=jnp.float32).astype(jnp.bfloat16)
    embedded_all = lax.all_gather(embedded, "tensor", axis=0, tiled=True)
    mixed_in = rms_scale(embedded_all, mix_gain)
    projected = jnp.einsum(
        "rd,jdc->jrc", mixed_in, in_proj, preferred_element_type=jnp.float32
    ).astype(jnp.bfloat16)
    slot_ids = jnp.arange(2 * context_count, dtype=jnp.int32)
    slot_pair = 2 * context_at + jnp.arange(2, dtype=jnp.int32)
    owned_blocks = jnp.sum(
        jnp.where(slot_ids[None, :] == slot_pair[:, None], block_order[None, :], 0), axis=1
    )
    local_pos = (
        owned_blocks[:, None] * block_rows + jnp.arange(block_rows, dtype=jnp.int32)[None, :]
    ).reshape(ctx_rows)
    tail_rows = jnp.stack(
        [projected[:, block_rows - halo_len : block_rows], projected[:, ctx_rows - halo_len :]]
    )
    all_tails = lax.all_gather(tail_rows, "context", axis=0, tiled=True)
    out_len = filter_len - 1 + block_rows
    pieces = []
    for block_at in range(2):
        holder_hit = (block_order == owned_blocks[block_at] - 1).astype(jnp.bfloat16)
        before_rows = jnp.einsum(
            "s,sjrc->jrc", holder_hit, all_tails, preferred_element_type=jnp.float32
        )
        own_rows = projected[:, block_at * block_rows : (block_at + 1) * block_rows].astype(
            jnp.float32
        )
        extended = jnp.concatenate([before_rows, own_rows], axis=1)
        filtered = short_conv(extended, short_filter, out_len)
        gated_rows = filtered[1] * filtered[2]
        padded = jnp.concatenate([jnp.zeros((1, chan_local), jnp.float32), gated_rows], axis=0)
        long_mix = long_conv(padded, long_filter, GROUP_CH)
        own_gate = gated_rows[filter_len - 1 :]
        pieces.append(
            (filtered[0, filter_len - 1 :] * (long_mix + conv_skip * own_gate)).astype(jnp.bfloat16)
        )
    hyena_mix = jnp.concatenate(pieces, axis=0)
    hyena_own = lax.psum_scatter(
        jnp.dot(hyena_mix, hyena_out, preferred_element_type=jnp.float32),
        "tensor",
        scatter_dimension=0,
        tiled=True,
    )
    stream_own = embedded.astype(jnp.float32) + hyena_own
    stream_all = lax.all_gather(stream_own, "tensor", axis=0, tiled=True)
    attn_in = rms_scale(stream_all, attn_gain)
    projections = jnp.einsum("rd,jdf->jrf", attn_in, qkv_proj, preferred_element_type=jnp.float32)
    local_heads = projections.shape[2] // HD
    shaped = projections.reshape(3, ctx_rows, local_heads, HD)
    queries = rotate(shaped[0], local_pos, HD).astype(jnp.bfloat16)
    keys_flat = (
        rotate(shaped[1], local_pos, HD).astype(jnp.bfloat16).reshape(ctx_rows, local_heads * HD)
    )
    values_flat = shaped[2].astype(jnp.bfloat16).reshape(ctx_rows, local_heads * HD)
    score_scale = HD ** (-0.5)
    start_state = (
        jnp.full((2, block_rows, local_heads), NEG_FILL, jnp.float32),
        jnp.zeros((2, block_rows, local_heads), jnp.float32),
        jnp.zeros((2, block_rows, local_heads, HD), jnp.float32),
    )
    key_piece = lax.all_gather(keys_flat, "context", axis=0, tiled=True)
    value_piece = lax.all_gather(values_flat, "context", axis=0, tiled=True)
    piece_len = key_piece.shape[0]
    sub_len = math.gcd(piece_len, 512)

    def attend_sub(sub_index, carried):
        key_block = lax.dynamic_slice_in_dim(key_piece, sub_index * sub_len, sub_len, 0).reshape(
            sub_len, local_heads, HD
        )
        value_block = lax.dynamic_slice_in_dim(
            value_piece, sub_index * sub_len, sub_len, 0
        ).reshape(sub_len, local_heads, HD)
        row_ids = sub_index * sub_len + jnp.arange(sub_len, dtype=jnp.int32)
        holder = row_ids // block_rows
        key_pos = (
            jnp.sum(
                jnp.where(holder[:, None] == slot_ids[None, :], block_order[None, :], 0), axis=1
            )
            * block_rows
            + row_ids % block_rows
        )
        top_all, sums_all, weighted_all = carried
        outputs = []
        for block_at in range(2):
            query_rows = queries[block_at * block_rows : (block_at + 1) * block_rows]
            query_pos = local_pos[block_at * block_rows : (block_at + 1) * block_rows]
            top_score = top_all[block_at]
            weight_sum = sums_all[block_at]
            weighted = weighted_all[block_at]
            scores = (
                jnp.einsum(
                    "qhd,khd->qhk", query_rows, key_block, preferred_element_type=jnp.float32
                )
                * score_scale
            )
            visible = key_pos[None, None, :] <= query_pos[:, None, None]
            scores = jnp.where(visible, scores, NEG_FILL)
            new_top = jnp.maximum(top_score, jnp.max(scores, axis=-1))
            rescale = jnp.exp(top_score - new_top)
            weights = jnp.where(visible, jnp.exp(scores - new_top[..., None]), 0.0)
            weight_sum = weight_sum * rescale + jnp.sum(weights, axis=-1)
            weighted = weighted * rescale[..., None] + jnp.einsum(
                "qhk,khd->qhd",
                weights.astype(jnp.bfloat16),
                value_block,
                preferred_element_type=jnp.float32,
            )
            result = (new_top, weight_sum, weighted)
            outputs.append(result)
        return tuple((jnp.stack([entry[field] for entry in outputs]) for field in range(3)))

    top_final, sums_final, weighted_final = lax.fori_loop(
        0, piece_len // sub_len, attend_sub, start_state
    )
    attended = (
        (weighted_final / sums_final[..., None])
        .astype(jnp.bfloat16)
        .reshape(ctx_rows, local_heads * HD)
    )
    attn_own = lax.psum_scatter(
        jnp.dot(attended, attn_out, preferred_element_type=jnp.float32).astype(jnp.bfloat16),
        "tensor",
        scatter_dimension=0,
        tiled=True,
    ).astype(jnp.float32)
    return stream_own + attn_own


def solution(mesh):
    placed = (
        P(("dp", "context", "tensor")),
        P("dp"),
        P(),
        P(),
        P(None, None, "tensor"),
        P(None, None, "tensor"),
        P("tensor", None),
        P("tensor"),
        P("tensor", None),
        P(),
        P(None, None, "tensor"),
        P("tensor", None),
    )
    return jax.shard_map(
        body,
        mesh=mesh,
        in_specs=placed,
        out_specs=P(("dp", "context", "tensor"), None),
        check_vma=False,
    )
```

profile of v0, /device:TPU:1, one launch (start us, length us, event | category | flops | bytes accessed | tf_op | source)
XLA Modules:
  0.0 769.6 jit_solution(17294564735795966699)
XLA Ops:
  6.5 3.9 convolution_convert_fusion.1
  10.5 51.8 %all-gather.7.cloned.1.call-done = bf16[512,4096]{1,0:T(8,128)(2,1)} async-done(((bf16[128,4096]{1,0:T(8,128)(2,1)}), bf16[512,4096]{1,0:T(8,128)(2,1)}) %all-gather.7.cloned.1.call-update) | async-done | bytes 4194320 | tf_op jit(solution)/shard_map/all_gather | solution.py:103
  65.8 9.9 %fusion.83 = bf16[3,512,512]{2,1,0:T(8,128)(2,1)S(1)} fusion(bf16[3,4096,512]{2,1,0:T(8,128)(2,1)} %param.20, bf16[512,4096]{1,0:T(8,128)(2,1)S(1)} %copy-done.10, f32[4096]{0:T(1024)S(1)} %copy-done.18, f32[512]{0:T(512)S(1)} %add_rsqrt_fusion.1), kind=kOutput, calls=%fused_computation.128 | convolution fusion | flops 6451625984 | bytes 18368512 | tf_op jit(solution)/shard_map/rd,jdc->jrc/dot_general | solution.py:105
  80.6 54.8 %gather_fusion.1 = f32[16384,32]{1,0:T(8,128)} fusion(f32[32,128]{0,1:T(8,128)S(1)} %copy.81, s32[16384]{0:T(1024)S(1)} %bitcast_clamp_fusion), kind=kCustom, calls=%fused_computation.1.clone | custom fusion | bytes 4259840 | tf_op jit(solution)/shard_map/jit(_take)/gather | solution.py:27
  135.4 6.5 copy.86
  141.9 54.8 %gather_fusion = f32[16384,32]{1,0:T(8,128)} fusion(f32[32,128]{0,1:T(8,128)S(1)} %copy.81, s32[16384]{0:T(1024)S(1)} %bitcast_clamp_fusion.1), kind=kCustom, calls=%fused_computation.clone | custom fusion | bytes 4259840 | tf_op jit(solution)/shard_map/jit(_take)/gather | solution.py:26
  196.7 5.5 copy.82
  202.3 3.4 slice_convert_fusion.2
  205.8 8.8 %fusion.38 = f32[1,3,129,512]{3,0,2,1:T(1,128)S(1)} fusion(bf16[32,3,129,512]{3,2,1,0:T(8,128)(2,1)} %all-gather.9.cloned.1.call-done, s32[32]{0:T(128)S(1)} %copy-done.14, s32[]{:T(128)} %bitcast.22), kind=kOutput, calls=%fused_computation.69 | convolution fusion | flops 12681248 | bytes 13473924 | tf_op jit(solution)/shard_map/s,sjrc->jrc/dot_general | solution.py:124
  214.6 3.7 fusion.40
  233.2 5.0 fusion.71
  238.2 3.4 fusion.89
  247.1 5.2 fusion.69
  257.3 4.6 fusion.95
  264.8 7.8 %fusion.120 = f32[512,4096]{1,0:T(8,128)} fusion(bf16[512,4096]{1,0:T(8,128)(2,1)} %param.24, bf16[256,512]{1,0:T(8,128)(2,1)S(1)} %get-tuple-element.361, bf16[256,512]{1,0:T(8,128)(2,1)S(1)} %get-tuple-element.360), kind=kOutput, calls=%fused_computation.170 | convolution fusion | flops 2148532224 | bytes 13107200 | tf_op jit(solution)/shard_map/dot_general | solution.py:141
  272.7 81.1 %reduce-scatter.3.cloned.1.call-done = f32[128,4096]{1,0:T(8,128)} async-done(((f32[512,4096]{1,0:T(8,128)}), f32[128,4096]{1,0:T(8,128)}) %reduce-scatter.3.cloned.1.call-update) | async-done | bytes 2097168 | tf_op jit(solution)/shard_map/reduce_scatter | solution.py:140
  357.6 82.3 %all-gather.11.cloned.1.call-done = f32[512,4096]{1,0:T(8,128)} async-done(((f32[128,4096]{1,0:T(8,128)}), f32[512,4096]{1,0:T(8,128)}) %all-gather.11.cloned.1.call-update) | async-done | bytes 8388624 | tf_op jit(solution)/shard_map/all_gather | solution.py:147
  439.9 4.2 multiply_reduce_fusion
  445.6 11.3 %fusion.77 = f32[3,512,512]{1,2,0:T(8,128)} fusion(bf16[3,4096,512]{2,1,0:T(8,128)(2,1)} %param.26, f32[512,4096]{1,0:T(8,128)S(1)} %copy-done.5, f32[4096]{0:T(1024)S(1)} %copy-done.19, f32[512]{0:T(512)S(1)} %add_rsqrt_fusion), kind=kOutput, calls=%fused_computation.126 | convolution fusion | flops 6448742400 | bytes 24135680 | tf_op jit(solution)/shard_map/rd,jdf->jrf/dot_general | solution.py:149
  462.5 75.8 %all-gather.13.cloned.1.call-done = bf16[8192,512]{0,1:T(8,128)(2,1)} async-done(((bf16[512,512]{0,1:T(8,128)(2,1)}), bf16[8192,512]{0,1:T(8,128)(2,1)}) %all-gather.13.cloned.1.call-update) | async-done | bytes 8388624 | tf_op jit(solution)/shard_map/all_gather | solution.py:163
  538.2 79.6 %all-gather.15.cloned.1.call-done = bf16[1,8192,512]{1,2,0:T(8,128)(2,1)} async-done(((bf16[1,512,512]{1,2,0:T(8,128)(2,1)}), bf16[1,8192,512]{1,2,0:T(8,128)(2,1)}) %all-gather.15.cloned.1.call-update) | async-done | bytes 8388624 | tf_op jit(solution)/shard_map/all_gather | solution.py:164
  618.0 87.3 %while.20 = (s32[]{:T(128)}, f32[2,256,4]{1,2,0:T(4,128)S(1)}, f32[2,256,4]{1,2,0:T(4,128)S(1)}, f32[2,256,4,128]{1,3,2,0:T(8,128)S(1)}, s32[32]{0:T(128)S(1)}, ...) while((s32[]{:T(128)}, f32[2,256,4]{1,2,0:T(4,128)S(1)}, ...), condition=%wide.region_10.12_spmd.clone, body=%wide.region_4.11_spmd.clone.sunk | while | flops 551627264 | bytes 22718784 | solution.py:214
  705.6 6.5 convolution_convert_fusion
  712.2 47.6 %reduce-scatter.5.cloned.1.call-done = bf16[128,4096]{1,0:T(8,128)(2,1)} async-done(((bf16[512,4096]{1,0:T(8,128)(2,1)}), bf16[128,4096]{1,0:T(8,128)(2,1)}) %reduce-scatter.5.cloned.1.call-update) | async-done | bytes 1048592 | tf_op jit(solution)/shard_map/reduce_scatter | solution.py:222
  (387 shorter events, 134.9 us)
Async XLA Ops:
  6.5 55.8 %all-gather.7.cloned.1.call-start = ((), (), s32[]{:S(2)}) async-start(), calls=%async_computation.2 | async-start | bytes 5242880 | tf_op jit(solution)/shard_map/all_gather | solution.py:103
  10.5 55.1 %copy-start.18 = (f32[4096]{0:T(1024)S(1)}, f32[4096]{0:T(1024)}, u32[]{:S(2)}) copy-start(f32[4096]{0:T(1024)} %param.19) | copy-start | bytes 49156
  10.5 195.3 %all-gather.9.cloned.1.call-start = ((), (), s32[]{:S(2)}) async-start(), calls=%async_computation.3 | async-start | bytes 14204928 | tf_op jit(solution)/shard_map/all_gather | solution.py:119
  62.3 3.4 copy-start.10
  76.8 1.6 copy-start.14
  76.8 3.6 copy-start.16
  76.9 3.6 copy-start.15
  78.1 275.6 %reduce-scatter.3.cloned.1.call-start = ((), (), s32[]{:S(2)}) async-start(), calls=%async_computation.4 | async-start | bytes 10485760 | tf_op jit(solution)/shard_map/reduce_scatter | solution.py:140
  205.8 8.8 %copy-start = (bf16[32,3,129,512]{3,2,1,0:T(8,128)(2,1)S(1)}, bf16[32,3,129,512]{3,2,1,0:T(8,128)(2,1)}, u32[]{:S(2)}) copy-start(bf16[32,3,129,512]{3,2,1,0:T(8,128)(2,1)} %all-gather.9.cloned.1.call-done) | copy-start | bytes 38043652
  218.3 1.4 copy-start.6
  218.3 1.9 copy-start.7
  222.3 1.4 copy-start.2
  222.3 2.4 copy-start.3
  233.2 5.0 copy-start.13
  247.1 5.2 copy-start.8
  261.9 1.3 copy-start.12
  272.6 81.2 %copy-start.4 = (bf16[128,4096]{1,0:T(8,128)(2,1)S(1)}, bf16[128,4096]{1,0:T(8,128)(2,1)}, u32[]{:S(2)}) copy-start(bf16[128,4096]{1,0:T(8,128)(2,1)} %convolution_convert_fusion.1) | copy-start | bytes 3145732
  272.6 167.3 %all-gather.11.cloned.1.call-start = ((), (), s32[]{:S(2)}) async-start(), calls=%async_computation.5 | async-start | bytes 10485760 | tf_op jit(solution)/shard_map/all_gather | solution.py:147
  356.9 181.4 %all-gather.13.cloned.1.call-start = ((), (), s32[]{:S(2)}) async-start(), calls=%async_computation.6 | async-start | bytes 8912896 | tf_op jit(solution)/shard_map/all_gather | solution.py:163
  357.0 87.0 %copy-start.19 = (f32[4096]{0:T(1024)S(1)}, f32[4096]{0:T(1024)}, u32[]{:S(2)}) copy-start(f32[4096]{0:T(1024)} %param.25) | copy-start | bytes 49156
  439.9 5.8 copy-start.5
  459.9 158.0 %all-gather.15.cloned.1.call-start = ((), (), s32[]{:S(2)}) async-start(), calls=%async_computation.8 | async-start | bytes 8912896 | tf_op jit(solution)/shard_map/all_gather | solution.py:164
  462.1 297.7 %reduce-scatter.5.cloned.1.call-start = ((), (), s32[]{:S(2)}) async-start(), calls=%async_computation.7 | async-start | bytes 5242880 | tf_op jit(solution)/shard_map/reduce_scatter | solution.py:222
  712.1 47.6 %copy-start.1 = (f32[128,4096]{1,0:T(8,128)S(1)}, f32[128,4096]{1,0:T(8,128)}, u32[]{:S(2)}) copy-start(f32[128,4096]{1,0:T(8,128)} %convert_add_fusion.1) | copy-start | bytes 6291460
  (3 other events, 3.6 us)
Sparse Core Ops, SparseCore 0:
  10.6 51.6 all-gather.6
  78.2 93.9 all-gather.8
  272.7 80.9 reduce-scatter.2
  357.0 82.8 all-gather.10
  460.0 78.1 all-gather.12
  540.2 77.6 all-gather.14
  712.3 47.4 reduce-scatter.4
where the time goes:
time: 775 us; the launch traced here: 770 us
  waiting for transfers between devices  418 us (54%)
  local copies, waits for them, and re-layouts  173 us (22%)
  matrix products  111 us (14%)
  other arithmetic  50.2 us (6%)
  between operations  15.3 us (2%)
    all_gather x1, waiting for transfers between devices, body(): stream_all = lax.all_gather(stream_own, 'tensor', axis=0, tiled=True)  82.3 us
    reduce_scatter x1, waiting for transfers between devices, body(): lax.psum_scatter(jnp.dot(hyena_mix, hyena_out, preferred_element_type=jnp...  81.1 us
    all_gather x1, waiting for transfers between devices, body(): value_piece = lax.all_gather(values_flat, 'context', axis=0, tiled=True)  79.6 us
    all_gather x1, waiting for transfers between devices, body(): key_piece = lax.all_gather(keys_flat, 'context', axis=0, tiled=True)  75.8 us
    gather x2, local copies, waits for them, and re-layouts, toeplitz(): jnp.take(long_filter, jnp.clip(tap_lag + filter_len, 0, filter_len - 1),...  61.2 us
    gather x2, local copies, waits for them, and re-layouts, toeplitz(): jnp.take(long_filter, jnp.clip(tap_lag, 0, filter_len - 1), axis=1)  60.3 us
    all_gather x1, waiting for transfers between devices, body(): embedded_all = lax.all_gather(embedded, 'tensor', axis=0, tiled=True)  51.8 us
    reduce_scatter x1, waiting for transfers between devices, body(): lax.psum_scatter(jnp.dot(attended, attn_out, preferred_element_type=jnp.f...  47.6 us
  transfers between devices with their start and end apart: 7, of which 6 were waited for; matrix products, arithmetic and copies ran while one was open for 17% of the time, Pallas kernels for 0%

commit v1 on v0

--- a/solution.py
+++ b/solution.py
@@ -161,7 +161,8 @@
         jnp.zeros((2, block_rows, local_heads, HD), jnp.float32),
     )
     key_piece = lax.all_gather(keys_flat, "context", axis=0, tiled=True)
-    value_piece = lax.all_gather(values_flat, "context", axis=0, tiled=True)
+    outgoing = jnp.stack([values_flat] * lax.axis_size("context"))
+    value_piece = jnp.concatenate(lax.all_to_all(outgoing, "context", 0, 0), axis=0)
     piece_len = key_piece.shape[0]
     sub_len = math.gcd(piece_len, 512)
 

time: 775 us -> 901 us (1.16)
  matrix products: 111 us -> 163 us
  local copies, waits for them, and re-layouts: 173 us -> 220 us
  other arithmetic: 50.2 us -> 68.2 us
    all_to_all x0 -> x1, waiting for transfers between devices: none -> 130 us  [body(): lax.all_to_all(outgoing, 'context', 0, 0)]
    all_gather x1 -> x0, waiting for transfers between devices: 79.6 us -> none  [body(): value_piece = lax.all_gather(values_flat, 'context', axis=0, tiled=True)]
    all_gather x1, waiting for transfers between devices: 75.8 us -> 26.1 us  [body(): key_piece = lax.all_gather(keys_flat, 'context', axis=0, tiled=True)]
    dynamic_slice x0 -> x32, local copies, waits for them, and re-layouts: none -> 33.4 us  [attend_sub(): lax.dynamic_slice_in_dim(value_piece, sub_index * sub_len, sub_len, 0)]
    dot_general x32, matrix products: 22.4 us -> 52.9 us  [attend_sub(): jnp.einsum('qhk,khd->qhd', weights.astype(jnp.bfloat16), value_block, pre...]
    dot_general x32, matrix products: 18.2 us -> 39.5 us  [attend_sub(): jnp.einsum('qhd,khd->qhk', query_rows, key_block, preferred_element_type=...]
    another operation x48, other arithmetic: 1.31 us -> 18.1 us  [attend_sub(): jnp.stack([entry[field] for entry in outputs])]
    all_to_all x0 -> x1, local copies, waits for them, and re-layouts: none -> 12.5 us  [body(): lax.all_to_all(outgoing, 'context', 0, 0)]
  transfers between devices with their start and end apart: 7 -> 7, of which waited for: 6 -> 6; matrix products, arithmetic and copies ran while one was open for 17% -> 16% of each run, Pallas kernels for 0% -> 0%
where the time goes in v1:
time: 901 us; the launch traced here: 895 us
  waiting for transfers between devices  420 us (47%)
  local copies, waits for them, and re-layouts  220 us (24%)
  matrix products  163 us (18%)
  other arithmetic  68.2 us (8%)
  between operations  15.4 us (2%)
    all_to_all x1, waiting for transfers between devices, body(): lax.all_to_all(outgoing, 'context', 0, 0)  130 us
    all_gather x1, waiting for transfers between devices, body(): stream_all = lax.all_gather(stream_own, 'tensor', axis=0, tiled=True)  82.3 us
    reduce_scatter x1, waiting for transfers between devices, body(): lax.psum_scatter(jnp.dot(hyena_mix, hyena_out, preferred_element_type=jnp...  81.1 us
    gather x2, local copies, waits for them, and re-layouts, toeplitz(): jnp.take(long_filter, jnp.clip(tap_lag + filter_len, 0, filter_len - 1),...  61.2 us
    gather x2, local copies, waits for them, and re-layouts, toeplitz(): jnp.take(long_filter, jnp.clip(tap_lag, 0, filter_len - 1), axis=1)  60.3 us
    dot_general x32, matrix products, attend_sub(): jnp.einsum('qhk,khd->qhd', weights.astype(jnp.bfloat16), value_block, pre...  52.9 us
    all_gather x1, waiting for transfers between devices, body(): embedded_all = lax.all_gather(embedded, 'tensor', axis=0, tiled=True)  51.8 us
    reduce_scatter x1, waiting for transfers between devices, body(): lax.psum_scatter(jnp.dot(attended, attn_out, preferred_element_type=jnp.f...  48.2 us
  transfers between devices with their start and end apart: 7, of which 6 were waited for; matrix products, arithmetic and copies ran while one was open for 16% of the time, Pallas kernels for 0%

profile of v1, /device:TPU:1, one launch (start us, length us, event | category | flops | bytes accessed | tf_op | source)
XLA Modules:
  0.0 894.7 jit_solution(18353546833112443424)
XLA Ops:
  6.5 3.9 convolution_convert_fusion.1
  10.5 51.8 %all-gather.5.cloned.1.call-done = bf16[512,4096]{1,0:T(8,128)(2,1)} async-done(((bf16[128,4096]{1,0:T(8,128)(2,1)}), bf16[512,4096]{1,0:T(8,128)(2,1)}) %all-gather.5.cloned.1.call-update) | async-done | bytes 4194320 | tf_op jit(solution)/shard_map/all_gather | solution.py:103
  65.8 9.9 %fusion.83 = bf16[3,512,512]{2,1,0:T(8,128)(2,1)S(1)} fusion(bf16[3,4096,512]{2,1,0:T(8,128)(2,1)} %param.20, bf16[512,4096]{1,0:T(8,128)(2,1)S(1)} %copy-done.12, f32[4096]{0:T(1024)S(1)} %copy-done.21, f32[512]{0:T(512)S(1)} %add_rsqrt_fusion.1), kind=kOutput, calls=%fused_computation.128 | convolution fusion | flops 6451625984 | bytes 18368512 | tf_op jit(solution)/shard_map/rd,jdc->jrc/dot_general | solution.py:105
  80.9 54.8 %gather_fusion.1 = f32[16384,32]{1,0:T(8,128)} fusion(f32[32,128]{0,1:T(8,128)S(1)} %copy.106, s32[16384]{0:T(1024)S(1)} %bitcast_clamp_fusion), kind=kCustom, calls=%fused_computation.1.clone | custom fusion | bytes 4259840 | tf_op jit(solution)/shard_map/jit(_take)/gather | solution.py:27
  135.7 6.5 copy.111
  142.2 54.8 %gather_fusion = f32[16384,32]{1,0:T(8,128)} fusion(f32[32,128]{0,1:T(8,128)S(1)} %copy.106, s32[16384]{0:T(1024)S(1)} %bitcast_clamp_fusion.1), kind=kCustom, calls=%fused_computation.clone | custom fusion | bytes 4259840 | tf_op jit(solution)/shard_map/jit(_take)/gather | solution.py:26
  196.9 5.5 copy.107
  206.0 8.8 fusion.38
  233.4 5.0 fusion.69
  247.3 5.2 fusion.71
  257.5 4.6 fusion.89
  265.0 7.8 fusion.121
  272.9 81.1 %reduce-scatter.3.cloned.1.call-done = f32[128,4096]{1,0:T(8,128)} async-done(((f32[512,4096]{1,0:T(8,128)}), f32[128,4096]{1,0:T(8,128)}) %reduce-scatter.3.cloned.1.call-update) | async-done | bytes 2097168 | tf_op jit(solution)/shard_map/reduce_scatter | solution.py:140
  357.8 82.3 %all-gather.9.cloned.1.call-done = f32[512,4096]{1,0:T(8,128)} async-done(((f32[128,4096]{1,0:T(8,128)}), f32[512,4096]{1,0:T(8,128)}) %all-gather.9.cloned.1.call-update) | async-done | bytes 8388624 | tf_op jit(solution)/shard_map/all_gather | solution.py:147
  440.1 4.2 multiply_reduce_fusion
  445.9 11.3 %fusion.77 = f32[3,512,512]{1,2,0:T(8,128)} fusion(bf16[3,4096,512]{2,1,0:T(8,128)(2,1)} %param.26, f32[512,4096]{1,0:T(8,128)S(1)} %copy-done.7, f32[4096]{0:T(1024)S(1)} %copy-done.22, f32[512]{0:T(512)S(1)} %add_rsqrt_fusion), kind=kOutput, calls=%fused_computation.126 | convolution fusion | flops 6448742400 | bytes 24135680 | tf_op jit(solution)/shard_map/rd,jdf->jrf/dot_general | solution.py:149
  461.5 4.1 stack.77
  465.6 6.6 all-to-all-start
  472.5 130.4 %all-to-all-done = bf16[16,512,512]{1,2,0:T(8,128)(2,1)} async-done(((bf16[16,512,512]{1,2,0:T(8,128)(2,1)}), bf16[16,512,512]{1,2,0:T(8,128)(2,1)}, u32[]{:S(2)}, u32[]{:S(2)}) %all-to-all-start) | async-done | bytes 8388640 | tf_op jit(solution)/shard_map/all_to_all | solution.py:165
  602.9 12.5 %copy.122 = bf16[16,512,512]{2,1,0:T(8,128)(2,1)} copy(bf16[16,512,512]{1,2,0:T(8,128)(2,1)} %all-to-all-done) | data formatting | bytes 16777216 | tf_op jit(solution)/shard_map/all_to_all | solution.py:165
  615.4 26.1 %all-gather.11.cloned.1.call-done = bf16[8192,512]{0,1:T(8,128)(2,1)} async-done(((bf16[512,512]{0,1:T(8,128)(2,1)}), bf16[8192,512]{0,1:T(8,128)(2,1)}) %all-gather.11.cloned.1.call-update) | async-done | bytes 8388624 | tf_op jit(solution)/shard_map/all_gather | solution.py:163
  642.6 186.0 %while.20 = (s32[]{:T(128)}, f32[2,256,4]{1,2,0:T(4,128)S(1)}, f32[2,256,4]{1,2,0:T(4,128)S(1)}, f32[2,256,4,128]{1,3,2,0:T(8,128)}, s32[32]{0:T(128)S(1)}, /*in...) while((s32[]{:T(128)}, f32[2,256,4]{1,2,0:T(4,128)S(1)}, ...), condition=%wide.region_10.12_spmd.clone, body=%wide.region_4.11_spmd.clone.sunk | while | flops 551627264 | bytes 38447504 | solution.py:215
  830.2 6.5 convolution_convert_fusion
  836.7 48.2 %reduce-scatter.5.cloned.1.call-done = bf16[128,4096]{1,0:T(8,128)(2,1)} async-done(((bf16[512,4096]{1,0:T(8,128)(2,1)}), bf16[128,4096]{1,0:T(8,128)(2,1)}) %reduce-scatter.5.cloned.1.call-update) | async-done | bytes 1048592 | tf_op jit(solution)/shard_map/reduce_scatter | solution.py:223
  (500 shorter events, 245.8 us)
Async XLA Ops:
  6.5 55.8 %all-gather.5.cloned.1.call-start = ((), (), s32[]{:S(2)}) async-start(), calls=%async_computation.3 | async-start | bytes 5242880 | tf_op jit(solution)/shard_map/all_gather | solution.py:103
  10.5 55.1 %copy-start.21 = (f32[4096]{0:T(1024)S(1)}, f32[4096]{0:T(1024)}, u32[]{:S(2)}) copy-start(f32[4096]{0:T(1024)} %param.19) | copy-start | bytes 49156
  10.5 195.5 %all-gather.7.cloned.1.call-start = ((), (), s32[]{:S(2)}) async-start(), calls=%async_computation.4 | async-start | bytes 14204928 | tf_op jit(solution)/shard_map/all_gather | solution.py:119
  62.4 3.4 copy-start.12
  76.9 3.8 copy-start.19
  76.9 3.9 copy-start.18
  78.1 275.8 %reduce-scatter.3.cloned.1.call-start = ((), (), s32[]{:S(2)}) async-start(), calls=%async_computation.5 | async-start | bytes 10485760 | tf_op jit(solution)/shard_map/reduce_scatter | solution.py:140
  206.0 8.8 copy-start.1
  233.4 5.0 copy-start.16
  247.3 5.2 copy-start.10
  272.8 81.2 %copy-start.6 = (bf16[128,4096]{1,0:T(8,128)(2,1)S(1)}, bf16[128,4096]{1,0:T(8,128)(2,1)}, u32[]{:S(2)}) copy-start(bf16[128,4096]{1,0:T(8,128)(2,1)} %convolution_convert_fusion.1) | copy-start | bytes 3145732
  272.8 167.3 %all-gather.9.cloned.1.call-start = ((), (), s32[]{:S(2)}) async-start(), calls=%async_computation.6 | async-start | bytes 10485760 | tf_op jit(solution)/shard_map/all_gather | solution.py:147
  357.1 284.4 %all-gather.11.cloned.1.call-start = ((), (), s32[]{:S(2)}) async-start(), calls=%async_computation.7 | async-start | bytes 8912896 | tf_op jit(solution)/shard_map/all_gather | solution.py:163
  357.3 87.0 %copy-start.22 = (f32[4096]{0:T(1024)S(1)}, f32[4096]{0:T(1024)}, u32[]{:S(2)}) copy-start(f32[4096]{0:T(1024)} %param.25) | copy-start | bytes 49156
  440.1 5.8 copy-start.7
  465.6 137.3 %all-to-all-start = ((bf16[16,512,512]{1,2,0:T(8,128)(2,1)}), bf16[16,512,512]{1,2,0:T(8,128)(2,1)}, u32[]{:S(2)}, u32[]{:S(2)}) async-start(bf16[16,512,512]{1,2,0:T(8,128)(2,1)} %stack.77), calls=%async_computation.1 | async-start | bytes 16777216 | tf_op jit(solution)/shard_map/all_to_all | solution.py:165
  472.1 412.8 %reduce-scatter.5.cloned.1.call-start = ((), (), s32[]{:S(2)}) async-start(), calls=%async_computation.8 | async-start | bytes 5242880 | tf_op jit(solution)/shard_map/reduce_scatter | solution.py:223
  648.7 2.6 copy-start.13
  660.3 2.6 copy-start.13
  683.5 2.6 copy-start.13
  695.2 2.6 copy-start.13
  718.4 2.6 copy-start.13
  730.0 2.6 copy-start.13
  836.7 48.2 %copy-start.2 = (f32[128,4096]{1,0:T(8,128)S(1)}, f32[128,4096]{1,0:T(8,128)}, u32[]{:S(2)}) copy-start(f32[128,4096]{1,0:T(8,128)} %convert_add_fusion.1) | copy-start | bytes 6291460
  (51 other events, 111.5 us)
Sparse Core Ops, SparseCore 0:
  10.6 51.6 all-gather.4
  78.3 93.9 all-gather.6
  273.0 80.9 reduce-scatter.2
  357.2 82.8 all-gather.8
  460.3 181.1 all-gather.10
  836.8 48.0 reduce-scatter.4
